TPU v7x, 256 devices: a whole 4x4x8 slice. The times are simulated.
256 devices in a mesh: prefix: 64 (over x, z, core), head: 4 (over y).
Axes of the slice: x: 4, y: 4, z: 8, core: 2. Of those that a mesh axis runs over, the one named last changes fastest.
Arguments:
- queries: bfloat16 [16384, 64, 128], P(('prefix', 'head')), may hold values from -8 to 8
- prefix_id: int32 [16384, 1], P(('prefix', 'head')), may hold values from 0 to 63; in each aligned block of 64 rows (0 to 63, 64 to 127, ...) at most 2 rows name the same one
- suffix_len: int32 [16384], P(('prefix', 'head')), may hold values from 2 to 32
- prefix_keys: bfloat16 [64, 2048, 8, 128], P('prefix', None, 'head'), may hold values from -8 to 8
- prefix_values: bfloat16 [64, 2048, 8, 128], P('prefix', None, 'head'), may hold values from -6 to 6
- suffix_keys: bfloat16 [16384, 32, 8, 128], P(('prefix', 'head')), may hold values from -8 to 8
- suffix_values: bfloat16 [16384, 32, 8, 128], P(('prefix', 'head')), may hold values from -6 to 6
- new_keys: bfloat16 [16384, 8, 128], P(('prefix', 'head')), may hold values from -8 to 8
- new_values: bfloat16 [16384, 8, 128], P(('prefix', 'head')), may hold values from -6 to 6
Outputs:
- attended: bfloat16 [16384, 64, 128], P(('prefix', 'head'))
Inputs may be any that keep to these rules, and one draw needn't show every extreme that they name: `prefix_id`: the 64 rows of one device name one prefix at most 2 times.
All inputs are finite; a program needn't handle non-finite values.
Results may differ from a plain program's by a relative error of at most 0.0036.
Values may be sent and summed in bfloat16 or wider, within the bound.
A program may use at most 64 MiB of HBM per device.

v0:
```python
import functools
import math

import jax
import jax.numpy as jnp
from jax import lax
from jax.experimental import pallas as pl
from jax.experimental.pallas import tpu as pltpu
from jax.sharding import PartitionSpec as P

MESH = pl.DeviceIdType.MESH
BF16 = jnp.bfloat16
F32 = jnp.float32
LOG2E = 1.4426950408889634
CAP = 2
PER_KV = 8
GROUP = 16
KEY_BLOCK = 256
TILE = 256
WINDOW = 4
PACK = 12


def axes_of(prefixes):
    return {64: (4, 8, 2)}[prefixes]


def step_offset(i, nz):
    odd = i % 2
    return odd * ((i + 1) // 2) + (1 - odd) * ((nz - i // 2) % nz)


def kernel(
    sizes,
    own_tab,
    row_i,
    row_n,
    suf_len,
    arrival,
    tab,
    q,
    kp_hbm,
    vp_hbm,
    sk_hbm,
    sv_hbm,
    nk,
    nv,
    out,
    spilled,
    out_a,
    in_a,
    out_b,
    in_b,
    out_bp,
    in_bp,
    out_ap,
    in_ap,
    out_m,
    in_m,
    out_mp,
    in_mp,
    in_tab,
    stab,
    out_f,
    in_f,
    rows_a,
    rows_bp,
    rows_m,
    sk,
    sv,
    kf,
    vf,
    stage,
    kc,
    vt,
    scores,
    sacc,
    smass,
    gath,
    pmt,
    load_sem,
    a_send,
    a_recv,
    b_send,
    b_recv,
    bp_send,
    bp_recv,
    m_send,
    m_recv,
    ap_send,
    ap_recv,
    mp_send,
    mp_recv,
    t_send,
    t_recv,
    f_sem,
):
    nx, nz, nc, ny = sizes
    plane = nx * nc * ny
    rows = q.shape[0]
    width = q.shape[-1]
    keys = kc.shape[0]
    scale = LOG2E / math.sqrt(width)
    me_p, y = lax.axis_index("prefix"), lax.axis_index("head")
    x, z, c = me_p // (nz * nc), (me_p // nc) % nz, me_p % nc

    def at(x_, z_, c_, y_):
        return ((x_ * nz + z_) * nc + c_, y_)

    def along_z(d):
        return at(x, (z + d) % nz, c, y)

    offsets = [(jx, jc, jy) for jx in range(nx) for jc in range(nc) for jy in range(ny)]
    y_at = [(y + jy) % ny for jy in range(ny)]
    column = {
        (sign, jx, jc): (((x + nx + sign * jx) % nx) * nz + z) * nc + (c + jc) % nc
        for sign in (1, -1)
        for jx in range(nx)
        for jc in range(nc)
    }

    def in_plane(j, sign):
        jx, jc, jy = offsets[j]
        return column[sign, jx, jc], y_at[sign * jy % ny]

    loads = [
        pltpu.make_async_copy(s, d, load_sem.at[n])
        for n, (s, d) in enumerate(((kp_hbm, kf), (vp_hbm, vf), (sk_hbm, sk), (sv_hbm, sv)))
    ]
    for load in loads:
        load.start()

    barrier = pltpu.get_barrier_semaphore()

    @pl.loop(1, nz)
    def _(d):
        pl.semaphore_signal(barrier, inc=1, device_id=along_z(d), device_id_type=MESH)

    for j in range(1, plane):
        pl.semaphore_signal(barrier, inc=1, device_id=in_plane(j, 1), device_id_type=MESH)

    pack = in_a.shape[1]

    def pack_a(i, dst):
        @pl.loop(0, pack, unroll=4)
        def _(n):
            row = own_tab[i, 0, 64 + n]
            for jy in range(ny):
                dst[i, n, jy] = q[row, y_at[jy]]

    pack_a(0, in_a)

    @pl.loop(1, nz)
    def _(i):
        pack_a(i, out_a)

    pl.semaphore_wait(barrier, nz - 1 + plane - 1)

    def a_copy(i):
        return pltpu.make_async_remote_copy(
            out_a.at[i], in_a.at[i], a_send.at[i], a_recv.at[i],
            device_id=along_z(step_offset(i, nz)), device_id_type=MESH,
        )

    def t_copy(i):
        return pltpu.make_async_remote_copy(
            tab.at[i], in_tab.at[i], t_send.at[i], t_recv.at[i],
            device_id=along_z(step_offset(i, nz)), device_id_type=MESH,
        )

    def start_b(i, table):
        rows_a[...] = in_a[i]

        @pl.loop(0, nx * nc, unroll=4)
        def _(k):
            for s in range(CAP):
                n = table[i, 0, k * CAP + s]
                for jy in range(ny):
                    out_b[i, k * ny + jy, s] = rows_a[n, jy]

        pltpu.make_async_copy(out_b.at[i, 0], in_b.at[i, 0], b_recv.at[i]).start()

        for j in range(1, plane):
            pltpu.make_async_remote_copy(
                out_b.at[i, j], in_b.at[i, j], b_send.at[i], b_recv.at[i],
                device_id=in_plane(j, 1), device_id_type=MESH,
            ).start()

    def start_bp(i, first, last):
        if first == 0:
            pltpu.make_async_copy(out_bp.at[i, 0], in_bp.at[i, 0], bp_recv.at[i]).start()
            pltpu.make_async_copy(out_m.at[i, 0], in_m.at[i, 0], m_recv.at[i]).start()
        for j in range(max(first, 1), last):
            pltpu.make_async_remote_copy(
                out_m.at[i, j // 4], in_m.at[i, j], m_send.at[i], m_recv.at[i],
                device_id=in_plane(j, -1), device_id_type=MESH,
            ).start()
            pltpu.make_async_remote_copy(
                out_bp.at[i, j], in_bp.at[i, j], bp_send.at[i], bp_recv.at[i],
                device_id=in_plane(j, -1), device_id_type=MESH,
            ).start()

    def ap_copies(i):
        back = along_z((nz - step_offset(i, nz)) % nz)
        return (
            pltpu.make_async_remote_copy(
                out_mp.at[i], in_mp.at[i], mp_send.at[i], mp_recv.at[i],
                device_id=back, device_id_type=MESH,
            ),
            pltpu.make_async_remote_copy(
                out_ap.at[i], in_ap.at[i], ap_send.at[i], ap_recv.at[i],
                device_id=back, device_id_type=MESH,
            ),
        )

    def wait_all(ref, sem):
        pltpu.make_async_copy(ref, ref, sem).wait()

    @pl.loop(1, nz)
    def _(i):
        t_copy(i).start()

    @pl.loop(1, 1 + WINDOW)
    def _(i):
        a_copy(i).start()

    pltpu.make_async_copy(tab.at[0], in_tab.at[0], t_recv.at[0]).start()
    start_b(0, own_tab)

    loads[0].wait()
    for part in range(2 * keys // 1024):
        stage[part * 1024 : (part + 1) * 1024] = kf[part * 1024 : (part + 1) * 1024].astype(F32)
    for part in range(keys // KEY_BLOCK):
        for k in range(2):
            block = stage[pl.ds(part * 2 * KEY_BLOCK + k, KEY_BLOCK, stride=2), :]
            kc[part * KEY_BLOCK : (part + 1) * KEY_BLOCK, k * width : (k + 1) * width] = block.astype(BF16)
    loads[1].wait()
    for part in range(2 * keys // 1024):
        stage[part * 1024 : (part + 1) * 1024] = vf[part * 1024 : (part + 1) * 1024].astype(F32)
    for part in range(keys // KEY_BLOCK):
        for k in range(2):
            block = stage[pl.ds(part * 2 * KEY_BLOCK + k, KEY_BLOCK, stride=2), :]
            vt[k * width : (k + 1) * width, part * KEY_BLOCK : (part + 1) * KEY_BLOCK] = block.T.astype(BF16)
    loads[2].wait()
    loads[3].wait()

    wait_all(in_tab.at[0], t_recv.at[0])

    @pl.loop(1, nz)
    def _(i):
        t_copy(i).wait()

    to_scalars = pltpu.make_async_copy(in_tab, stab, f_sem.at[0])
    to_scalars.start()
    worst = in_tab[0]
    for i in range(1, nz):
        worst = jnp.maximum(worst, in_tab[i])
    out_f[...] = worst
    in_f[0] = worst

    for j in range(1, plane):
        pltpu.make_async_remote_copy(
            out_f, in_f.at[j], f_sem.at[1], f_sem.at[2],
            device_id=in_plane(j, 1), device_id_type=MESH,
        ).start()

    to_scalars.wait()

    kv = nk.shape[1]
    cols = sk.shape[1]
    heads = ny * GROUP
    head_of = lax.broadcasted_iota(jnp.int32, (heads, cols), 0) // PER_KV
    col = lax.broadcasted_iota(jnp.int32, (heads, cols), 1)
    own_head = head_of == col % kv

    def suffix_row(r):
        qr = q[r].reshape(heads, width)
        s = lax.dot_general(qr, sk[r], (((1,), (1,)), ((), ())), preferred_element_type=F32)
        s = jnp.where(own_head & (col < suf_len[r] * kv), s * scale, -1e30)
        new_k = jnp.broadcast_to(nk[r].astype(F32)[:, None, :], (kv, PER_KV, width)).reshape(heads, width)
        new_v = jnp.broadcast_to(nv[r].astype(F32)[:, None, :], (kv, PER_KV, width)).reshape(heads, width)
        own = jnp.sum(qr.astype(F32) * new_k, axis=1, keepdims=True) * scale
        top = jnp.maximum(jnp.max(s, axis=1, keepdims=True), own)
        w = jnp.exp2(s - top)
        own_w = jnp.exp2(own - top)
        total = jnp.sum(w, axis=1, keepdims=True) + own_w
        acc = jnp.dot(w.astype(BF16), sv[r], preferred_element_type=F32)
        acc = acc + own_w.astype(BF16).astype(F32) * new_v
        sacc[r] = (acc / total).reshape(ny, GROUP, width)
        smass[r] = jnp.broadcast_to(top + jnp.log2(total), (heads, width)).reshape(ny, GROUP, width)

    part_rows = rows // nz

    def suffix_part(i):
        @pl.loop(0, part_rows // 2)
        def _(n):
            suffix_row(i * part_rows + 2 * n)
            suffix_row(i * part_rows + 2 * n + 1)

    low_row = lax.broadcasted_iota(jnp.int32, (TILE, width), 0) % GROUP < PER_KV
    low_lane = lax.broadcasted_iota(jnp.int32, (width, TILE), 1) % GROUP < PER_KV
    senders = TILE // (CAP * GROUP)

    blocks = [slice(b, b + KEY_BLOCK) for b in range(0, keys, KEY_BLOCK)]

    def score(i, t):
        xq = in_b[i, t * senders : (t + 1) * senders].reshape(TILE, width).astype(F32)
        xq = jnp.concatenate(
            [jnp.where(low_row, xq, 0.0), jnp.where(low_row, 0.0, xq)], axis=1
        ).astype(BF16)
        top = None
        for block in blocks:
            s = lax.dot_general(kc[block], xq, (((1,), (1,)), ((), ())), preferred_element_type=F32)
            scores[t % 2, block] = s
            high = jnp.max(s, axis=0, keepdims=True)
            top = high if top is None else jnp.maximum(top, high)
        return top * scale

    def weigh(i, t, top):
        total = jnp.zeros_like(top)
        acc = jnp.zeros((2 * width, TILE), F32)
        for block in blocks:
            w = jnp.exp2(scores[t % 2, block] * scale - top)
            total = total + jnp.sum(w, axis=0, keepdims=True)
            acc = acc + jnp.dot(vt[:, block], w.astype(BF16), preferred_element_type=F32)
        o = jnp.where(low_lane, acc[:width], acc[width:]) / total
        out_bp[i, t * senders : (t + 1) * senders] = o.T.astype(BF16).reshape(senders, CAP, GROUP, width)
        mass = top + jnp.log2(total)
        for h in range(TILE // 128):
            out_m[i, t * (TILE // 128) + h] = mass[:, h * 128 : (h + 1) * 128]

    def attend(i):
        tiles = plane // senders
        top = score(i, 0)
        for t in range(tiles):
            later = score(i, t + 1) if t + 1 < tiles else None
            weigh(i, t, top)
            start_bp(i, t * senders, (t + 1) * senders)
            top = later

    mass_lane = lax.broadcasted_iota(jnp.int32, (1, 128), 1)

    def give_back(i):
        wait_all(in_bp.at[i], bp_recv.at[i])
        wait_all(in_m.at[i], m_recv.at[i])
        rows_bp[...] = in_bp[i]
        rows_m[...] = in_m[i]

        @pl.loop(0, pack, unroll=4)
        def _(n):
            k, slot = stab[i, 0, 16 + n], stab[i, 0, 32 + n]
            mass = rows_m[k * ny]
            for jy in range(ny):
                out_ap[i, n, jy] = rows_bp[k * ny + jy, slot]
                if jy > 0:
                    mass = jnp.where(mass_lane // (CAP * GROUP) == jy, rows_m[k * ny + jy], mass)
            out_mp[i, n] = mass


    suffix_part(0)
    suffix_part(1)
    wait_all(in_b.at[0], b_recv.at[0])
    attend(0)

    @pl.loop(1, nz + 2)
    def _(n):
        @pl.when(n < nz)
        def _():
            a_copy(n).wait_recv()
            start_b(n, stab)

        @pl.when(n + WINDOW < nz)
        def _():
            a_copy(n + WINDOW).start()

        @pl.when(n <= nz // 2 - 1)
        def _():
            suffix_part(2 * n)
            suffix_part(2 * n + 1)

        @pl.when((n >= 2) & (n <= nz))
        def _():
            wait_all(in_b.at[n - 1], b_recv.at[n - 1])
            attend(n - 1)

        @pl.when(n == 1)
        def _():
            give_back(0)
            pltpu.make_async_copy(out_mp.at[0], in_mp.at[0], mp_recv.at[0]).start()
            pltpu.make_async_copy(out_ap.at[0], in_ap.at[0], ap_recv.at[0]).start()

        @pl.when(n >= 3)
        def _():
            give_back(n - 2)
            for copy in ap_copies(n - 2):
                copy.start()

    wait_all(in_f.at[pl.ds(1, plane - 1)], f_sem.at[1])
    wait_all(in_f.at[pl.ds(1, plane - 1)], f_sem.at[2])
    spilled[0] = jnp.max(jnp.where(mass_lane == 48, jnp.max(in_f[...], axis=0), 0))
    wait_all(in_b.at[0, pl.ds(1, plane - 1)], b_send.at[0])
    wait_all(in_bp.at[0, pl.ds(1, plane - 1)], bp_send.at[0])
    wait_all(in_m.at[0, pl.ds(1, plane - 1)], m_send.at[0])
    wait_all(in_mp.at[0], mp_recv.at[0])
    wait_all(in_ap.at[0], ap_recv.at[0])

    @pl.loop(1, nz)
    def _(i):
        a_copy(i).wait_send()
        wait_all(in_b.at[i, pl.ds(1, plane - 1)], b_send.at[i])
        wait_all(in_bp.at[i, pl.ds(1, plane - 1)], bp_send.at[i])
        wait_all(in_m.at[i, pl.ds(1, plane - 1)], m_send.at[i])
        for copy in ap_copies(i):
            copy.wait()

    @pl.loop(0, rows, unroll=8)
    def _(r):
        gath[pl.ds(r, 1), :] = in_mp[row_i[r], row_n[r]]

    turned = gath[...].T
    for jy in range(ny):
        first = turned[jy * 32 : jy * 32 + GROUP]
        second = turned[jy * 32 + GROUP : jy * 32 + 2 * GROUP]
        pmt[jy] = jnp.where(arrival[...] == 0, first, second)

    lane = lax.broadcasted_iota(jnp.int32, (GROUP, rows), 1)

    def merge_row(r):
        i, n = row_i[r], row_n[r]
        for jy in range(ny):
            yy = y_at[jy]
            pm = jnp.sum(jnp.where(lane == r, pmt[jy], 0.0), axis=1, keepdims=True)
            gap = smass[r, yy] - pm
            e = jnp.exp2(-jnp.abs(gap))
            ahead = gap <= 0
            po = in_ap[i, n, jy].astype(F32)
            so = sacc[r, yy]
            merged = (jnp.where(ahead, 1.0, e) * po + jnp.where(ahead, e, 1.0) * so) / (1.0 + e)
            out[r, yy] = merged.astype(BF16)

    @pl.loop(0, rows // 2)
    def _(n):
        merge_row(2 * n)
        merge_row(2 * n + 1)


def wide_attend(received, key_cache, value_cache, scale_factor):
    lined = jnp.transpose(received, (3, 1, 0, 2, 4, 5))

    def per_head(packed_tuple):
        head_query, head_keys, head_values = packed_tuple

        def per_group(block_query_rows):
            scores = (
                jnp.einsum(
                    "ncgd,td->ncgt", block_query_rows, head_keys, preferred_element_type=jnp.float32
                )
                * scale_factor
            )
            highest = jnp.max(scores, axis=-1)
            weights_raw = jnp.exp(scores - highest[..., None])
            totals = jnp.sum(weights_raw, axis=-1)
            blended = jnp.einsum(
                "ncgt,td->ncgd",
                weights_raw.astype(jnp.bfloat16),
                head_values,
                preferred_element_type=jnp.float32,
            )
            return ((blended / totals[..., None]).astype(jnp.bfloat16), highest + jnp.log(totals))

        return lax.map(per_group, head_query)

    blended, log_mass = lax.map(
        per_head,
        (lined, jnp.transpose(key_cache, (1, 0, 2)), jnp.transpose(value_cache, (1, 0, 2))),
    )
    return (jnp.transpose(blended, (2, 1, 3, 0, 4, 5)), jnp.transpose(log_mass, (2, 1, 3, 0, 4)))


def wide_body(
    queries,
    prefix_id,
    suffix_len,
    prefix_keys,
    prefix_values,
    suffix_keys,
    suffix_values,
    new_keys,
    new_values,
):
    row_count, head_count, head_width = queries.shape
    kv_all = suffix_keys.shape[2]
    per_kv = head_count // kv_all
    owners = lax.axis_size("prefix")
    capacity = 2 * row_count // owners
    scale_factor = 1.0 / math.sqrt(head_width)
    target = prefix_id[:, 0]
    row_index = lax.broadcasted_iota(jnp.int32, (row_count, row_count), 0)
    col_index = lax.broadcasted_iota(jnp.int32, (row_count, row_count), 1)
    earlier = (target[None, :] == target[:, None]) & (col_index < row_index)
    arrival = jnp.sum(earlier.astype(jnp.int32), axis=1)
    position = target * capacity + arrival
    query_layout = queries.reshape(row_count, kv_all, per_kv, head_width)
    outbox = (
        jnp.zeros((owners * capacity, kv_all, per_kv, head_width), jnp.bfloat16)
        .at[position]
        .set(query_layout)
    )
    outbox = outbox.reshape(owners, 1, capacity, kv_all, per_kv, head_width)
    key_cache = prefix_keys[0]
    value_cache = prefix_values[0]
    received = lax.all_to_all(
        lax.all_to_all(outbox, "prefix", split_axis=0, concat_axis=0, tiled=True),
        "head",
        split_axis=3,
        concat_axis=1,
        tiled=True,
    )
    blended, log_mass = wide_attend(received, key_cache, value_cache, scale_factor)
    blended = lax.all_to_all(
        lax.all_to_all(blended, "prefix", split_axis=0, concat_axis=0, tiled=True),
        "head",
        split_axis=1,
        concat_axis=3,
        tiled=True,
    )
    log_mass = lax.all_to_all(
        lax.all_to_all(log_mass, "prefix", split_axis=0, concat_axis=0, tiled=True),
        "head",
        split_axis=1,
        concat_axis=3,
        tiled=True,
    )
    prefix_out = blended.reshape(owners * capacity, kv_all, per_kv, head_width)[position].astype(
        jnp.float32
    )
    prefix_mass = log_mass.reshape(owners * capacity, kv_all, per_kv)[position]
    private_scores = (
        jnp.einsum("wtfb,wmtb->wtfm", query_layout, suffix_keys, preferred_element_type=jnp.float32)
        * scale_factor
    )
    visible = (jnp.arange(suffix_keys.shape[1], dtype=jnp.int32)[None, :] < suffix_len[:, None])[
        :, None, None, :
    ]
    private_scores = jnp.where(visible, private_scores, -jnp.inf)
    own_score = (
        jnp.einsum("rkgd,rkd->rkg", query_layout, new_keys, preferred_element_type=jnp.float32)
        * scale_factor
    )
    suffix_top = jnp.maximum(jnp.max(private_scores, axis=-1), own_score)
    suffix_raw = jnp.where(visible, jnp.exp(private_scores - suffix_top[..., None]), 0.0)
    own_weight = jnp.exp(own_score - suffix_top)
    suffix_totals = jnp.sum(suffix_raw, axis=-1) + own_weight
    gathered = jnp.einsum(
        "rkgs,rskd->rkgd",
        suffix_raw.astype(jnp.bfloat16),
        suffix_values,
        preferred_element_type=jnp.float32,
    )
    gathered = (
        gathered
        + own_weight.astype(jnp.bfloat16).astype(jnp.float32)[..., None]
        * new_values.astype(jnp.float32)[:, :, None, :]
    )
    suffix_out = gathered / suffix_totals[..., None]
    suffix_mass = suffix_top + jnp.log(suffix_totals)
    ceiling = jnp.maximum(prefix_mass, suffix_mass)
    share_prefix = jnp.exp(prefix_mass - ceiling)
    share_suffix = jnp.exp(suffix_mass - ceiling)
    merged = (share_prefix[..., None] * prefix_out + share_suffix[..., None] * suffix_out) / (
        share_prefix + share_suffix
    )[..., None]
    return merged.reshape(row_count, head_count, head_width).astype(jnp.bfloat16)


def body(
    queries,
    prefix_id,
    suffix_len,
    prefix_keys,
    prefix_values,
    suffix_keys,
    suffix_values,
    new_keys,
    new_values,
):
    rows, heads, width = queries.shape
    prefixes, ny = lax.axis_size("prefix"), lax.axis_size("head")
    nx, nz, nc = axes_of(prefixes)
    plane = nx * nc * ny
    keys = prefix_keys.shape[1]
    slots, kv = suffix_keys.shape[1:3]

    me_p = lax.axis_index("prefix")
    x, z, c = me_p // (nz * nc), (me_p // nc) % nz, me_p % nc
    target = prefix_id[:, 0]
    dz = (target // nc - z) % nz
    step = jnp.where(dz == 0, 0, jnp.where(2 * dz <= nz, 2 * dz - 1, 2 * (nz - dz)))
    spot = ((target // (nz * nc) - x) % nx) * nc + (target - c) % nc
    r_index = lax.broadcasted_iota(jnp.int32, (rows, rows), 0)
    c_index = lax.broadcasted_iota(jnp.int32, (rows, rows), 1)
    earlier = c_index < r_index
    arrival = jnp.sum(((target[None, :] == target[:, None]) & earlier).astype(jnp.int32), axis=1)
    rank = jnp.sum(((step[None, :] == step[:, None]) & earlier).astype(jnp.int32), axis=1)
    row_n = jnp.minimum(rank, PACK - 1)
    spill = (rank >= PACK).astype(jnp.int32)
    shape = (nz, 128, rows)
    t_step = lax.broadcasted_iota(jnp.int32, shape, 0)
    t_lane = lax.broadcasted_iota(jnp.int32, shape, 1)
    field, entry = t_lane // 16, t_lane % 16
    mine = (step[None, None, :] == t_step) & (spill == 0)[None, None, :]
    by_slot = mine & ((spot * CAP + arrival)[None, None, :] == entry)
    by_rank = mine & (rank[None, None, :] == entry)
    r_value = lax.broadcasted_iota(jnp.int32, shape, 2)
    value = jnp.where((field == 0) & by_slot, rank[None, None, :], 0)
    value = jnp.where((field == 1) & by_rank, spot[None, None, :], value)
    value = jnp.where((field == 2) & by_rank, arrival[None, None, :], value)
    value = jnp.where((field == 3) & (entry == 0), spill[None, None, :], value)
    value = jnp.where((field == 4) & by_rank, r_value, value)
    table = jnp.sum(value, axis=2)[:, None, :]

    smem = pl.BlockSpec(memory_space=pltpu.SMEM)
    vmem = pl.BlockSpec(memory_space=pltpu.VMEM)
    hbm = pl.BlockSpec(memory_space=pl.ANY)
    message = (CAP, GROUP, width)
    dma = pltpu.SemaphoreType.DMA
    attended, spilled = pl.pallas_call(
        functools.partial(kernel, (nx, nz, nc, ny)),
        out_shape=(
            jax.ShapeDtypeStruct((rows, ny, GROUP, width), BF16),
            jax.ShapeDtypeStruct((1,), jnp.int32),
        ),
        in_specs=[smem] * 4 + [vmem] * 3 + [hbm] * 4 + [vmem] * 2,
        out_specs=(vmem, smem),
        scratch_shapes=[
            pltpu.VMEM((nz, PACK, ny, GROUP, width), BF16),
            pltpu.VMEM((nz, PACK, ny, GROUP, width), BF16),
            pltpu.VMEM((nz, plane) + message, BF16),
            pltpu.VMEM((nz, plane) + message, BF16),
            pltpu.VMEM((nz, plane) + message, BF16),
            pltpu.VMEM((nz, plane) + message, BF16),
            pltpu.VMEM((nz, PACK, ny, GROUP, width), BF16),
            pltpu.VMEM((nz, PACK, ny, GROUP, width), BF16),
            pltpu.VMEM((nz, plane // 4, 1, 128), F32),
            pltpu.VMEM((nz, plane, 1, 128), F32),
            pltpu.VMEM((nz, PACK, 1, 128), F32),
            pltpu.VMEM((nz, PACK, 1, 128), F32),
            pltpu.VMEM((nz, 1, 128), jnp.int32),
            pltpu.SMEM((nz, 1, 128), jnp.int32),
            pltpu.VMEM((1, 128), jnp.int32),
            pltpu.VMEM((plane, 1, 128), jnp.int32),
            pltpu.VMEM((PACK, ny, GROUP, width), BF16),
            pltpu.VMEM((plane,) + message, BF16),
            pltpu.VMEM((plane, 1, 128), F32),
            pltpu.VMEM((rows, slots * kv, width), BF16),
            pltpu.VMEM((rows, slots * kv, width), BF16),
            pltpu.VMEM((2 * keys, width), BF16),
            pltpu.VMEM((2 * keys, width), BF16),
            pltpu.VMEM((2 * keys, width), F32),
            pltpu.VMEM((keys, 2 * width), BF16),
            pltpu.VMEM((2 * width, keys), BF16),
            pltpu.VMEM((2, keys, TILE), F32),
            pltpu.VMEM((rows, ny, GROUP, width), F32),
            pltpu.VMEM((rows, ny, GROUP, width), F32),
            pltpu.VMEM((rows, 128), F32),
            pltpu.VMEM((ny, GROUP, rows), F32),
            dma((4,)),
        ]
        + [dma((nz,))] * 14
        + [dma((3,))],
        compiler_params=pltpu.CompilerParams(
            collective_id=0, has_side_effects=True, vmem_limit_bytes=56 * 2**20
        ),
    )(
        table,
        step,
        row_n,
        suffix_len,
        arrival[None, :],
        table,
        queries.reshape(rows, ny, GROUP, width),
        prefix_keys.reshape(2 * keys, width),
        prefix_values.reshape(2 * keys, width),
        suffix_keys.reshape(rows, slots * kv, width),
        suffix_values.reshape(rows, slots * kv, width),
        new_keys,
        new_values,
    )
    args = (
        queries,
        prefix_id,
        suffix_len,
        prefix_keys,
        prefix_values,
        suffix_keys,
        suffix_values,
        new_keys,
        new_values,
    )
    return lax.cond(
        spilled[0] > 0,
        wide_body,
        lambda *_: attended.reshape(rows, heads, width),
        *args,
    )


def solution(mesh):
    rows = P(("prefix", "head"))
    cache = P("prefix", None, "head", None)
    return jax.shard_map(
        body,
        mesh=mesh,
        in_specs=(rows, rows, rows, cache, cache, rows, rows, rows, rows),
        out_specs=rows,
        check_vma=False,
    )
```

profile of v0, /device:TPU:1, one launch (start us, length us, event | category | flops | bytes accessed | tf_op | source)
XLA Modules:
  0.0 119.9 jit_solution(10892735560967402627)
XLA Ops:
  0.0 0.9 convert_reduce_fusion.1
  0.9 0.0 copy-start.12
  1.0 0.7 multiply_add_fusion
  1.6 0.0 copy-start.13
  1.7 0.7 fusion.65
  2.3 0.2 convert_reduce_fusion.2
  2.6 0.9 select_reduce_fusion
  3.4 0.6 broadcast_minimum_fusion.row_n
  4.0 0.0 copy-done.12
  4.0 0.0 copy-done.13
  4.0 0.0 copy-start.2
  4.0 0.0 copy-start.17
  4.0 112.8 %shard_map.93 = (bf16[64,4,16,128]{3,2,1,0:T(8,128)(2,1)}, s32[1]{0:T(128)}) custom-call(s32[8,1,128]{2,1,0:T(1,128)} %bitcast.146, s32[64]{0:T(128)} %copy-done.13, s32[64]{0:T(128)} %broadcast_minimum_fusion.row_n, s32[64]{0:T(128)} %suf_len.1, s32[1,64]{1,0:T(1,128)} %bitcast.148, s32[8,1,128]{2,1,0:T(1,128)} %bitcast.147, ...), custom_call_target="tpu_custom_call" | custom-call | tf_op jit(solution)/shard_map/pallas_call | solution.py:627
  117.4 0.0 copy-done.2
  117.4 0.0 copy-done.17
  117.4 0.2 conditional.1
  117.6 2.3 %copy.183 = bf16[64,64,128]{2,1,0:T(8,128)(2,1)} copy(bf16[64,64,128]{2,1,0:T(8,128)(2,1)} %get-tuple-element.106) | data formatting | bytes 2097152
  (4 shorter events, 0.0 us)
Async XLA Ops:
  0.9 3.1 %copy-start.12 = (s32[64]{0:T(128)}, s32[64]{0:T(128)S(1)}, u32[]{:S(2)}) copy-start(s32[64]{0:T(128)S(1)} %convert_reduce_fusion.1) | copy-start | bytes 772
  1.6 2.4 %copy-start.13 = (s32[64]{0:T(128)}, s32[64]{0:T(128)S(1)}, u32[]{:S(2)}) copy-start(s32[64]{0:T(128)S(1)} %get-tuple-element.263.row_i) | copy-start | bytes 772
  4.0 113.4 %copy-start.2 = (bf16[64,64,128]{2,1,0:T(8,128)(2,1)S(1)}, bf16[64,64,128]{2,1,0:T(8,128)(2,1)}, u32[]{:S(2)}) copy-start(bf16[64,64,128]{2,1,0:T(8,128)(2,1)} %param.15) | copy-start | bytes 3145732
  4.0 113.4 %copy-start.17 = (s32[64,1]{0,1:T(1,128)S(1)}, s32[64,1]{0,1:T(1,128)}, u32[]{:S(2)}) copy-start(s32[64,1]{0,1:T(1,128)} %param.16) | copy-start | bytes 772
where the time goes:
time: 120 us
  Pallas kernels  113 us (94%)
  other arithmetic  3.9 us (3%)
  local copies, waits for them, and re-layouts  2.28 us (2%)
    pallas_call x1, Pallas kernels, body(): pl.pallas_call(functools.partial(kernel, (nx, nz, nc, ny)), out_shape=(ja...  113 us

commit v1 on v0

--- a/solution.py
+++ b/solution.py
@@ -17,7 +17,7 @@
 GROUP = 16
 KEY_BLOCK = 256
 TILE = 256
-WINDOW = 4
+WINDOW = 7
 PACK = 12
 
 
@@ -186,31 +186,33 @@
                 device_id=in_plane(j, 1), device_id_type=MESH,
             ).start()
 
+    def start_m(g):
+        pltpu.make_async_copy(out_m.at[g, 0], in_m.at[g, 0], m_recv.at[g]).start()
+        for j in range(1, plane):
+            pltpu.make_async_remote_copy(
+                out_m.at[g, j // 4], in_m.at[g, j], m_send.at[g], m_recv.at[g],
+                device_id=in_plane(j, -1), device_id_type=MESH,
+            ).start()
+
     def start_bp(i, first, last):
         if first == 0:
             pltpu.make_async_copy(out_bp.at[i, 0], in_bp.at[i, 0], bp_recv.at[i]).start()
-            pltpu.make_async_copy(out_m.at[i, 0], in_m.at[i, 0], m_recv.at[i]).start()
         for j in range(max(first, 1), last):
-            pltpu.make_async_remote_copy(
-                out_m.at[i, j // 4], in_m.at[i, j], m_send.at[i], m_recv.at[i],
-                device_id=in_plane(j, -1), device_id_type=MESH,
-            ).start()
             pltpu.make_async_remote_copy(
                 out_bp.at[i, j], in_bp.at[i, j], bp_send.at[i], bp_recv.at[i],
                 device_id=in_plane(j, -1), device_id_type=MESH,
             ).start()
 
-    def ap_copies(i):
-        back = along_z((nz - step_offset(i, nz)) % nz)
-        return (
-            pltpu.make_async_remote_copy(
-                out_mp.at[i], in_mp.at[i], mp_send.at[i], mp_recv.at[i],
-                device_id=back, device_id_type=MESH,
-            ),
-            pltpu.make_async_remote_copy(
-                out_ap.at[i], in_ap.at[i], ap_send.at[i], ap_recv.at[i],
-                device_id=back, device_id_type=MESH,
-            ),
+    def ap_copy(i):
+        return pltpu.make_async_remote_copy(
+            out_ap.at[i], in_ap.at[i], ap_send.at[i], ap_recv.at[i],
+            device_id=along_z((nz - step_offset(i, nz)) % nz), device_id_type=MESH,
+        )
+
+    def mp_copy(i):
+        return pltpu.make_async_remote_copy(
+            out_mp.at[i], in_mp.at[i], mp_send.at[i], mp_recv.at[i],
+            device_id=along_z((nz - step_offset(i, nz)) % nz), device_id_type=MESH,
         )
 
     def wait_all(ref, sem):
@@ -327,7 +329,7 @@
         out_bp[i, t * senders : (t + 1) * senders] = o.T.astype(BF16).reshape(senders, CAP, GROUP, width)
         mass = top + jnp.log2(total)
         for h in range(TILE // 128):
-            out_m[i, t * (TILE // 128) + h] = mass[:, h * 128 : (h + 1) * 128]
+            out_m[i // 2, t * (TILE // 128) + h, i % 2] = mass[:, h * 128 : (h + 1) * 128]
 
     def attend(i):
         tiles = plane // senders
@@ -340,21 +342,29 @@
 
     mass_lane = lax.broadcasted_iota(jnp.int32, (1, 128), 1)
 
+    def give_masses(g):
+        wait_all(in_m.at[g], m_recv.at[g])
+        rows_m[...] = in_m[g]
+        for h in range(2):
+            i = 2 * g + h
+
+            @pl.loop(0, pack, unroll=4)
+            def _(n):
+                k = stab[i, 0, 16 + n]
+                mass = rows_m[k * ny, h]
+                for jy in range(1, ny):
+                    mass = jnp.where(mass_lane // (CAP * GROUP) == jy, rows_m[k * ny + jy, h], mass)
+                out_mp[i, n] = mass
+
     def give_back(i):
         wait_all(in_bp.at[i], bp_recv.at[i])
-        wait_all(in_m.at[i], m_recv.at[i])
         rows_bp[...] = in_bp[i]
-        rows_m[...] = in_m[i]
 
         @pl.loop(0, pack, unroll=4)
         def _(n):
             k, slot = stab[i, 0, 16 + n], stab[i, 0, 32 + n]
-            mass = rows_m[k * ny]
             for jy in range(ny):
                 out_ap[i, n, jy] = rows_bp[k * ny + jy, slot]
-                if jy > 0:
-                    mass = jnp.where(mass_lane // (CAP * GROUP) == jy, rows_m[k * ny + jy], mass)
-            out_mp[i, n] = mass
 
 
     suffix_part(0)
@@ -383,24 +393,39 @@
             wait_all(in_b.at[n - 1], b_recv.at[n - 1])
             attend(n - 1)
 
+            @pl.when(n % 2 == 0)
+            def _():
+                start_m((n - 1) // 2)
+
         @pl.when(n == 1)
         def _():
             give_back(0)
-            pltpu.make_async_copy(out_mp.at[0], in_mp.at[0], mp_recv.at[0]).start()
             pltpu.make_async_copy(out_ap.at[0], in_ap.at[0], ap_recv.at[0]).start()
 
         @pl.when(n >= 3)
         def _():
             give_back(n - 2)
-            for copy in ap_copies(n - 2):
-                copy.start()
+            ap_copy(n - 2).start()
+
+        @pl.when((n >= 3) & (n % 2 == 1))
+        def _():
+            g = (n - 3) // 2
+            give_masses(g)
+            mp_copy(2 * g + 1).start()
+
+            @pl.when(g > 0)
+            def _():
+                mp_copy(2 * g).start()
+
+            @pl.when(g == 0)
+            def _():
+                pltpu.make_async_copy(out_mp.at[0], in_mp.at[0], mp_recv.at[0]).start()
 
     wait_all(in_f.at[pl.ds(1, plane - 1)], f_sem.at[1])
     wait_all(in_f.at[pl.ds(1, plane - 1)], f_sem.at[2])
     spilled[0] = jnp.max(jnp.where(mass_lane == 48, jnp.max(in_f[...], axis=0), 0))
     wait_all(in_b.at[0, pl.ds(1, plane - 1)], b_send.at[0])
     wait_all(in_bp.at[0, pl.ds(1, plane - 1)], bp_send.at[0])
-    wait_all(in_m.at[0, pl.ds(1, plane - 1)], m_send.at[0])
     wait_all(in_mp.at[0], mp_recv.at[0])
     wait_all(in_ap.at[0], ap_recv.at[0])
 
@@ -409,13 +434,16 @@
         a_copy(i).wait_send()
         wait_all(in_b.at[i, pl.ds(1, plane - 1)], b_send.at[i])
         wait_all(in_bp.at[i, pl.ds(1, plane - 1)], bp_send.at[i])
-        wait_all(in_m.at[i, pl.ds(1, plane - 1)], m_send.at[i])
-        for copy in ap_copies(i):
-            copy.wait()
+        ap_copy(i).wait()
+        mp_copy(i).wait()
+
+    @pl.loop(0, nz // 2)
+    def _(g):
+        wait_all(in_m.at[g, pl.ds(1, plane - 1)], m_send.at[g])
 
     @pl.loop(0, rows, unroll=8)
     def _(r):
-        gath[pl.ds(r, 1), :] = in_mp[row_i[r], row_n[r]]
+        gath[pl.ds(r, 1), :] = in_mp[row_i[r], jnp.minimum(row_n[r], pack - 1)]
 
     turned = gath[...].T
     for jy in range(ny):
@@ -426,7 +454,7 @@
     lane = lax.broadcasted_iota(jnp.int32, (GROUP, rows), 1)
 
     def merge_row(r):
-        i, n = row_i[r], row_n[r]
+        i, n = row_i[r], jnp.minimum(row_n[r], pack - 1)
         for jy in range(ny):
             yy = y_at[jy]
             pm = jnp.sum(jnp.where(lane == r, pmt[jy], 0.0), axis=1, keepdims=True)
@@ -602,7 +630,6 @@
     earlier = c_index < r_index
     arrival = jnp.sum(((target[None, :] == target[:, None]) & earlier).astype(jnp.int32), axis=1)
     rank = jnp.sum(((step[None, :] == step[:, None]) & earlier).astype(jnp.int32), axis=1)
-    row_n = jnp.minimum(rank, PACK - 1)
     spill = (rank >= PACK).astype(jnp.int32)
     shape = (nz, 128, rows)
     t_step = lax.broadcasted_iota(jnp.int32, shape, 0)
@@ -641,8 +668,8 @@
             pltpu.VMEM((nz, plane) + message, BF16),
             pltpu.VMEM((nz, PACK, ny, GROUP, width), BF16),
             pltpu.VMEM((nz, PACK, ny, GROUP, width), BF16),
-            pltpu.VMEM((nz, plane // 4, 1, 128), F32),
-            pltpu.VMEM((nz, plane, 1, 128), F32),
+            pltpu.VMEM((nz // 2, plane // 4, 2, 1, 128), F32),
+            pltpu.VMEM((nz // 2, plane, 2, 1, 128), F32),
             pltpu.VMEM((nz, PACK, 1, 128), F32),
             pltpu.VMEM((nz, PACK, 1, 128), F32),
             pltpu.VMEM((nz, 1, 128), jnp.int32),
@@ -651,7 +678,7 @@
             pltpu.VMEM((plane, 1, 128), jnp.int32),
             pltpu.VMEM((PACK, ny, GROUP, width), BF16),
             pltpu.VMEM((plane,) + message, BF16),
-            pltpu.VMEM((plane, 1, 128), F32),
+            pltpu.VMEM((plane, 2, 1, 128), F32),
             pltpu.VMEM((rows, slots * kv, width), BF16),
             pltpu.VMEM((rows, slots * kv, width), BF16),
             pltpu.VMEM((2 * keys, width), BF16),
@@ -674,7 +701,7 @@
     )(
         table,
         step,
-        row_n,
+        rank,
         suffix_len,
         arrival[None, :],
         table,

time: 120 us -> 119 us (level)
  no operation moved by 1% of the time
where the time goes in v1:
time: 119 us
  Pallas kernels  112 us (94%)
  other arithmetic  3.32 us (3%)
  local copies, waits for them, and re-layouts  2.29 us (2%)
    pallas_call x1, Pallas kernels, body(): pl.pallas_call(functools.partial(kernel, (nx, nz, nc, ny)), out_shape=(ja...  112 us

profile of v1, /device:TPU:1, one launch (start us, length us, event | category | flops | bytes accessed | tf_op | source)
XLA Modules:
  0.0 118.9 jit_solution(1056941023293485644)
XLA Ops:
  0.0 0.9 convert_reduce_fusion.1
  0.9 0.0 copy-start.12
  1.0 0.7 multiply_add_fusion
  1.6 0.0 copy-start.13
  1.7 0.7 fusion.65
  2.3 0.2 convert_reduce_fusion.2.row_n
  2.5 0.0 copy-start.15
  2.6 0.9 select_reduce_fusion
  3.4 0.0 copy-done.12
  3.4 0.0 copy-done.13
  3.4 0.0 copy-done.15
  3.4 0.0 copy-start.2
  3.4 0.0 copy-start.18
  3.5 112.3 %shard_map.93 = (bf16[64,4,16,128]{3,2,1,0:T(8,128)(2,1)}, s32[1]{0:T(128)}) custom-call(s32[8,1,128]{2,1,0:T(1,128)} %bitcast.146, s32[64]{0:T(128)} %copy-done.13, s32[64]{0:T(128)} %copy-done.15, s32[64]{0:T(128)} %suf_len.1, s32[1,64]{1,0:T(1,128)} %bitcast.148, s32[8,1,128]{2,1,0:T(1,128)} %bitcast.147, bf16[64,4,16,128]{3,2,1,0:T(8,128)(2,1)} %bitcast.134, ...), custom_call_target="tpu_custom_call" | custom-call | tf_op jit(solution)/shard_map/pallas_call | solution.py:654
  116.4 0.0 copy-done.2
  116.4 0.0 copy-done.18
  116.4 0.2 conditional.1
  116.6 2.3 %copy.183 = bf16[64,64,128]{2,1,0:T(8,128)(2,1)} copy(bf16[64,64,128]{2,1,0:T(8,128)(2,1)} %get-tuple-element.106) | data formatting | bytes 2097152
  (4 shorter events, 0.0 us)
Async XLA Ops:
  0.9 2.5 %copy-start.12 = (s32[64]{0:T(128)}, s32[64]{0:T(128)S(1)}, u32[]{:S(2)}) copy-start(s32[64]{0:T(128)S(1)} %convert_reduce_fusion.1) | copy-start | bytes 772
  1.6 1.8 %copy-start.13 = (s32[64]{0:T(128)}, s32[64]{0:T(128)S(1)}, u32[]{:S(2)}) copy-start(s32[64]{0:T(128)S(1)} %get-tuple-element.263.row_i) | copy-start | bytes 772
  2.5 0.9 copy-start.15
  3.4 112.9 %copy-start.2 = (bf16[64,64,128]{2,1,0:T(8,128)(2,1)S(1)}, bf16[64,64,128]{2,1,0:T(8,128)(2,1)}, u32[]{:S(2)}) copy-start(bf16[64,64,128]{2,1,0:T(8,128)(2,1)} %param.15) | copy-start | bytes 3145732
  3.4 112.9 %copy-start.18 = (s32[64,1]{0,1:T(1,128)S(1)}, s32[64,1]{0,1:T(1,128)}, u32[]{:S(2)}) copy-start(s32[64,1]{0,1:T(1,128)} %param.16) | copy-start | bytes 772
